TPU v7x, 256 devices: a whole 4x4x8 slice. The times are simulated.
256 devices in a mesh: row: 8 (over y, core), col: 32 (over z, x).
Axes of the slice: x: 4, y: 4, z: 8, core: 2. Of those that a mesh axis runs over, the one named last changes fastest.
Arguments:
- tokens: bfloat16 [2048, 8192], P('row', 'col'), may hold values from -500 to 500
- norm_gain: float32 [8192], replicated, may hold values from 0.1 to 1.9
- gate_weight: bfloat16 [8192, 28672], P('row', 'col'), may hold values from -0.0625 to 0.0625
- up_weight: bfloat16 [8192, 28672], P('row', 'col'), may hold values from -0.0625 to 0.0625
- down_weight: bfloat16 [28672, 8192], P('col', 'row'), may hold values from -0.03125 to 0.03125
Outputs:
- mixed: bfloat16 [2048, 8192], P('col', 'row')
All inputs are finite; a program needn't handle non-finite values.
Results may differ from a plain program's by a relative error of at most 0.034.
Values may be sent and summed in bfloat16 or wider, within the bound.
A program may use at most 64 MiB of HBM per device.

v0:
```python
import jax
import jax.numpy as jnp
from jax import lax
from jax.sharding import PartitionSpec as P

D = 8192


EPSILON = 1e-05


def local(tokens, norm_gain, gate_weight, up_weight, down_weight):
    width = tokens.shape[1]
    values = tokens.astype(jnp.float32)
    squares = lax.psum(jnp.sum(values * values, axis=1), "col")
    factor = lax.rsqrt(squares / D + EPSILON)
    offset = lax.axis_index("col") * width
    local_gain = lax.dynamic_slice_in_dim(norm_gain, offset, width, 0)
    normed = (values * factor[:, None] * local_gain[None, :]).astype(jnp.bfloat16)
    features = lax.all_gather(normed, "col", axis=1, tiled=True)
    columns = lax.all_to_all(features, "row", split_axis=1, concat_axis=0, tiled=True)
    hidden_width = gate_weight.shape[1]
    gate_term = jnp.dot(columns, gate_weight, preferred_element_type=jnp.float32)
    up_term = jnp.dot(columns, up_weight, preferred_element_type=jnp.float32)
    totals = lax.psum_scatter(
        jnp.concatenate([gate_term, up_term], axis=1).astype(jnp.bfloat16),
        "row",
        scatter_dimension=0,
        tiled=True,
    ).astype(jnp.float32)
    hidden = (jax.nn.silu(totals[:, :hidden_width]) * totals[:, hidden_width:]).astype(jnp.bfloat16)
    partial_value = jnp.dot(
        lax.all_gather(hidden, "row", axis=0, tiled=True),
        down_weight,
        preferred_element_type=jnp.float32,
    )
    mixed = lax.psum_scatter(
        partial_value.astype(jnp.bfloat16), "col", scatter_dimension=0, tiled=True
    )
    return mixed


def solution(mesh):
    return jax.shard_map(
        local,
        mesh=mesh,
        in_specs=(P("row", "col"), P(), P("row", "col"), P("row", "col"), P("col", "row")),
        out_specs=P("col", "row"),
        check_vma=False,
    )
```

profile of v0, /device:TPU:1, one launch (start us, length us, event | category | flops | bytes accessed | tf_op | source)
XLA Modules:
  0.0 563.9 jit_solution(1752292834480291070)
XLA Ops:
  6.5 0.0 copy-start
  6.5 0.0 all-gather.3.cloned.1.call-start
  6.5 1.1 copy.6
  7.7 0.1 fusion.1
  7.7 64.3 %psum.7 = f32[256]{0:T(256)S(1)} all-reduce(f32[256]{0:T(256)S(1)} %fusion.1), channel_id=1, replica_groups=mesh['row'=8,'col'=32] {'col'}, use_global_device_ids=true, to_apply=%region_1.0 | all-reduce | flops 256 | bytes 2048 | tf_op jit(solution)/shard_map/psum | solution.py:15
  72.1 0.8 dynamic_slice.3
  72.8 0.8 fusion.3
  73.6 0.0 all-gather.3.cloned.1.call-update
  73.6 0.0 reduce-scatter.3.cloned.1.call-start
  73.7 88.2 %all-gather.3.cloned.1.call-done = bf16[256,8192]{0,1:T(8,128)(2,1)} async-done(((bf16[256,256]{0,1:T(8,128)(2,1)}), bf16[256,8192]{0,1:T(8,128)(2,1)}) %all-gather.3.cloned.1.call-update) | async-done | bytes 4194320 | tf_op jit(solution)/shard_map/all_gather | solution.py:20
  161.9 57.1 %all_to_all.19 = bf16[256,8,1024]{0,2,1:T(8,128)(2,1)} all-to-all(bf16[256,8,1024]{0,2,1:T(8,128)(2,1)} %bitcast.10), channel_id=1, replica_groups=mesh['row'=8,'col'=32] {'row'}, dimensions={1} | all-to-all | bytes 8388608 | tf_op jit(solution)/shard_map/all_to_all | solution.py:21
  218.9 6.5 %copy.7 = bf16[8,256,1024]{2,1,0:T(8,128)(2,1)} copy(bf16[8,256,1024]{1,2,0:T(8,128)(2,1)} %bitcast.9) | data formatting | bytes 8388608 | tf_op jit(solution)/shard_map/all_to_all | solution.py:21
  225.4 0.0 copy-start.1
  225.4 0.0 copy-start.2
  225.4 8.8 %convolution_convert_fusion.1 = bf16[2048,896]{0,1:T(8,128)(2,1)} fusion(bf16[2048,1024]{1,0:T(8,128)(2,1)} %bitcast.11, bf16[1024,896]{1,0:T(8,128)(2,1)} %param.8), kind=kOutput, calls=%fused_computation.2 | convolution fusion | flops 3759931392 | bytes 9699328 | tf_op jit(solution)/shard_map/dot_general | solution.py:24
  234.3 0.0 copy-done.1
  234.3 0.0 copy-done.2
  234.3 5.5 convolution_convert_fusion.2
  239.8 7.5 %pad_maximum_fusion = bf16[2048,1792]{0,1:T(8,128)(2,1)} fusion(bf16[2048,896]{0,1:T(8,128)(2,1)} %convolution_convert_fusion.1, bf16[2048,896]{0,1:T(8,128)(2,1)} %convolution_convert_fusion.2), kind=kLoop, calls=%fused_computation | loop fusion | flops 14680064 | bytes 14680064 | tf_op jit(solution)/shard_map/concatenate | solution.py:26
  247.3 0.0 reduce-scatter.3.cloned.1.call-update
  247.3 0.0 all-gather.5.cloned.1.call-start
  247.3 45.4 %reduce-scatter.3.cloned.1.call-done = bf16[256,1792]{0,1:T(8,128)(2,1)} async-done(((bf16[2048,1792]{0,1:T(8,128)(2,1)}), bf16[256,1792]{0,1:T(8,128)(2,1)}) %reduce-scatter.3.cloned.1.call-update) | async-done | bytes 917520 | tf_op jit(solution)/shard_map/reduce_scatter | solution.py:25
  292.7 1.3 convert_element_type.18
  294.1 1.1 fusion
  295.1 0.0 all-gather.5.cloned.1.call-update
  295.1 0.0 reduce-scatter.5.cloned.1.call-start
  295.2 37.1 %all-gather.5.cloned.1.call-done = bf16[2048,896]{0,1:T(8,128)(2,1)} async-done(((bf16[256,896]{0,1:T(8,128)(2,1)}), bf16[2048,896]{0,1:T(8,128)(2,1)}) %all-gather.5.cloned.1.call-update) | async-done | bytes 3670032 | tf_op jit(solution)/shard_map/all_gather | solution.py:33
  332.3 0.0 copy-done
  332.3 8.2 %convolution_convert_fusion = bf16[2048,1024]{1,0:T(8,128)(2,1)} fusion(bf16[2048,896]{0,1:T(8,128)(2,1)} %all-gather.5.cloned.1.call-done, bf16[896,1024]{1,0:T(8,128)(2,1)S(1)} %copy-done), kind=kOutput, calls=%fused_computation.1 | convolution fusion | flops 3760193536 | bytes 9699328 | tf_op jit(solution)/shard_map/dot_general | solution.py:32
  340.6 0.0 reduce-scatter.5.cloned.1.call-update
  340.6 216.8 %reduce-scatter.5.cloned.1.call-done = bf16[64,1024]{1,0:T(8,128)(2,1)} async-done(((bf16[2048,1024]{1,0:T(8,128)(2,1)}), bf16[64,1024]{1,0:T(8,128)(2,1)}) %reduce-scatter.5.cloned.1.call-update) | async-done | bytes 131088 | tf_op jit(solution)/shard_map/reduce_scatter | solution.py:37
  (1 shorter events, 0.0 us)
Async XLA Ops:
  6.5 325.8 %copy-start = (bf16[896,1024]{1,0:T(8,128)(2,1)S(1)}, bf16[896,1024]{1,0:T(8,128)(2,1)}, u32[]{:S(2)}) copy-start(bf16[896,1024]{1,0:T(8,128)(2,1)} %param.9) | copy-start | bytes 5505028
  6.5 155.3 %all-gather.3.cloned.1.call-start = ((), (), s32[]{:S(2)}) async-start(), calls=%async_computation.3 | async-start | bytes 4325376 | tf_op jit(solution)/shard_map/all_gather | solution.py:20
  73.6 219.1 %reduce-scatter.3.cloned.1.call-start = ((), (), s32[]{:S(2)}) async-start(), calls=%async_computation.4 | async-start | bytes 8257536 | tf_op jit(solution)/shard_map/reduce_scatter | solution.py:25
  225.4 8.8 %copy-start.1 = (bf16[8,256,1024]{2,1,0:T(8,128)(2,1)S(1)}, bf16[8,256,1024]{2,1,0:T(8,128)(2,1)}, u32[]{:S(2)}) copy-start(bf16[8,256,1024]{2,1,0:T(8,128)(2,1)} %copy.7) | copy-start | bytes 12582916
  225.4 8.8 %copy-start.2 = (bf16[1024,896]{1,0:T(8,128)(2,1)S(1)}, bf16[1024,896]{1,0:T(8,128)(2,1)}, u32[]{:S(2)}) copy-start(bf16[1024,896]{1,0:T(8,128)(2,1)} %param.7) | copy-start | bytes 5505028
  247.3 85.0 %all-gather.5.cloned.1.call-start = ((), (), s32[]{:S(2)}) async-start(), calls=%async_computation.5 | async-start | bytes 4128768 | tf_op jit(solution)/shard_map/all_gather | solution.py:33
  295.1 262.3 %reduce-scatter.5.cloned.1.call-start = ((), (), s32[]{:S(2)}) async-start(), calls=%async_computation.6 | async-start | bytes 4325376 | tf_op jit(solution)/shard_map/reduce_scatter | solution.py:37
Sparse Core Ops, SparseCore 0:
  73.7 88.1 all-gather.2
  247.4 45.2 reduce-scatter.2
  295.3 37.0 all-gather.4
  340.7 216.6 reduce-scatter.4
where the time goes:
time: 569 us; the launch traced here: 564 us
  waiting for transfers between devices  388 us (68%)
  blocking collectives  121 us (21%)
  matrix products  22.6 us (4%)
  between operations  13.2 us (2%)
  other arithmetic  10.7 us (2%)
  local copies, waits for them, and re-layouts  8.4 us (1%)
    reduce_scatter x1, waiting for transfers between devices, local(): lax.psum_scatter(partial_value.astype(jnp.bfloat16), 'col', scatter_dimen...  217 us
    all_gather x1, waiting for transfers between devices, local(): features = lax.all_gather(normed, 'col', axis=1, tiled=True)  88.2 us
    psum x1, blocking collectives, local(): squares = lax.psum(jnp.sum(values * values, axis=1), 'col')  64.3 us
    all_to_all x1, blocking collectives, local(): lax.all_to_all(features, 'row', split_axis=1, concat_axis=0, tiled=True)  57.1 us
    reduce_scatter x1, waiting for transfers between devices, local(): lax.psum_scatter(jnp.concatenate([gate_term, up_term], axis=1).astype(jnp...  45.4 us
    all_gather x1, waiting for transfers between devices, local(): lax.all_gather(hidden, 'row', axis=0, tiled=True)  37.1 us
  transfers between devices with their start and end apart: 4, of which 4 were waited for; matrix products, arithmetic and copies ran while one was open for 0% of the time, Pallas kernels for 0%

commit v1 on v0

v1 whole, which is shorter than its diff:
```python
import functools

import jax
import jax.numpy as jnp
from jax import lax
from jax.experimental import pallas as pl
from jax.experimental.pallas import tpu as pltpu
from jax.sharding import PartitionSpec as P

D = 8192
EPSILON = 1e-05
BF16 = jnp.bfloat16
F32 = jnp.float32

PARTS = 4
S = 64 // PARTS
M = 4 * S
LAG = 4
COPIES = 200


def kernel(
    tok_ref, gain_ref, gate_hbm, up_hbm, down_hbm, out_ref,
    w, wd, st, xs, g, pr, yl, yf, comb, h, o, zl, xl, xd, xf, zb, ss, sx, sz, fb,
    wsem, send_sems, recv_sems,
):
    row = lax.axis_index("row")
    col = lax.axis_index("col")
    y, k = lax.div(row, 2), lax.rem(row, 2)
    z, x = lax.div(col, 4), lax.rem(col, 4)

    def at(ax=0, ay=0, az=0):
        yy = lax.rem(y + ay + 4, 4)
        zz = lax.rem(z + az + 8, 8)
        xx = lax.rem(x + ax + 4, 4)
        return (2 * yy + k, 4 * zz + xx)

    partner = (2 * y + 1 - k, col)
    across = (z, 4 * row + x)
    stays = row == z

    barrier = pltpu.get_barrier_semaphore()

    def greet(device):
        pl.semaphore_signal(barrier, inc=1, device_id=device, device_id_type=pl.DeviceIdType.MESH)

    others = [at(ax=1), at(ax=2), at(ax=3), at(ay=1), at(ay=3), partner]
    others += [at(az=i) for i in range(1, 8)]
    for device in others:
        greet(device)

    loads = [
        pltpu.make_async_copy(gate_hbm, w.at[:, 0:896], wsem.at[0]),
        pltpu.make_async_copy(up_hbm, w.at[:, 896:1792], wsem.at[1]),
        pltpu.make_async_copy(down_hbm, wd, wsem.at[2]),
    ]
    for load in loads:
        load.start()

    @pl.when(jnp.logical_not(stays))
    def _():
        greet(across)

    count = [0]
    started = []

    def make(src, dst, device):
        index = count[0]
        count[0] += 1
        return pltpu.make_async_remote_copy(
            src_ref=src, dst_ref=dst,
            send_sem=send_sems.at[index], recv_sem=recv_sems.at[index],
            device_id=device, device_id_type=pl.DeviceIdType.MESH,
        )

    def send(src, dst, device):
        copy = make(src, dst, device)
        copy.start()
        started.append(copy)
        return copy

    def slot(r):
        r = lax.rem(r + 16, 8)
        return 4 * lax.rem(r, 2) + lax.div(r, 2)

    def piece(xx):
        xx = lax.rem(xx + 8, 4)
        return pl.ds(pl.multiple_of(xx * 256, 256), 256)

    values = tok_ref[...].astype(F32)
    scaled = (values * gain_ref[pl.ds(col, 1), :]).astype(BF16)
    for j in range(PARTS):
        st[j] = scaled[:, j * S:(j + 1) * S, :].reshape(M, 256)
    flat = values.reshape(256, 256)
    squares = jnp.sum(flat * flat, axis=1, keepdims=True)
    diagonal = lax.broadcasted_iota(jnp.int32, (256, 256), 0) == lax.broadcasted_iota(jnp.int32, (256, 256), 1)
    ss[0] = jnp.broadcast_to(jnp.sum(jnp.where(diagonal, squares, 0.0), axis=0, keepdims=True), (8, 256))

    @pl.when(stays)
    def _():
        pl.semaphore_wait(barrier, 13)

    @pl.when(jnp.logical_not(stays))
    def _():
        pl.semaphore_wait(barrier, 14)

    moves = [make(st.at[j], xs.at[j, slot(row), :, piece(x)], across) for j in range(PARTS)]

    @pl.when(jnp.logical_not(stays))
    def _():
        for move in moves:
            move.start()

    @pl.when(stays)
    def _():
        for j in range(PARTS):
            xs[j, slot(row), :, piece(x)] = st[j]

    def arrive(j):
        @pl.when(jnp.logical_not(stays))
        def _():
            moves[j].wait_recv()

    def norm():
        sends = [send(ss.at[0], sx.at[i - 1], at(ax=i)) for i in (1, 2, 3)]
        yield
        yield
        for copy in sends:
            copy.wait_recv()
        ss[1] = ss[0] + sx[0] + sx[1] + sx[2]
        sends = [send(ss.at[1], sz.at[i - 1], at(az=i)) for i in range(1, 8)]
        yield
        yield
        for copy in sends:
            copy.wait_recv()
        total = ss[1]
        for i in range(7):
            total = total + sz[i]
        factor = lax.rsqrt(total[0:1, :] / D + EPSILON)
        column = jnp.sum(jnp.where(diagonal, factor, 0.0), axis=1, keepdims=True)
        fb[...] = jnp.broadcast_to(column, (256, 128)).reshape(4, 64, 128)

    def ring_gather(view, half):
        right = send(view(z), view(z), at(az=1))
        left = send(view(z), view(z), at(az=-1))
        yield
        for step in (1, 2, 3):
            right.wait_recv()
            src = view(z - step) if step < 3 else half(z - step, 0)
            next_right = send(src, src, at(az=1))
            left.wait_recv()
            src = view(z + step) if step < 3 else half(z + step, 1)
            next_left = send(src, src, at(az=-1))
            right, left = next_right, next_left
            yield
        right.wait_recv()
        left.wait_recv()

    def gather_wide_z(j):
        block = xs.at[j, slot(z), :, piece(x)]
        sends = [send(block, block, at(ax=i)) for i in (1, 3, 2)]
        yield
        for copy in sends:
            copy.wait_recv()
        yield from ring_gather(
            lambda zz: xs.at[j, slot(zz)],
            lambda zz, i: xs.at[j, slot(zz), pl.ds(i * (M // 2), M // 2)],
        )

    def gather_wide_x(j):
        yield from ring_gather(
            lambda zz: xs.at[j, slot(zz), :, piece(x)],
            lambda zz, i: xs.at[j, slot(zz), pl.ds(i * (M // 2), M // 2), piece(x)],
        )
        block = xs.at[j, :, :, piece(x)]
        right = send(block, block, at(ax=1))
        left = send(block, block, at(ax=-1))
        yield
        right.wait_recv()
        block = xs.at[j, 0:4, :, piece(x - 1)]
        right = send(block, block, at(ax=1))
        left.wait_recv()
        block = xs.at[j, 4:8, :, piece(x + 1)]
        left = send(block, block, at(ax=-1))
        yield
        right.wait_recv()
        left.wait_recv()

    def gate_up(j, part):
        first = part * 4
        rows = xs.at[j, pl.ds(first, 4)]

        def tile(n, carry):
            cols = pl.ds(pl.multiple_of(n * 256, 256), 256)
            result = jnp.dot(rows[...].reshape(4 * M, 1024), w[:, cols], preferred_element_type=F32)
            g[j, pl.ds(first, 4), :, cols] = result.astype(BF16).reshape(4, M, 256)
            return carry

        lax.fori_loop(0, 7, tile, 0)

    def down(j, part):
        first = part * 4
        rows = h.at[j, pl.ds(first, 4)]

        def tile(n, carry):
            cols = pl.ds(pl.multiple_of(n * 256, 256), 256)
            result = jnp.dot(rows[...].reshape(4 * M, 896), wd[:, cols], preferred_element_type=F32)
            o[j, pl.ds(first, 4), :, :, cols] = result.astype(BF16).reshape(4, 4, S, 256)
            return carry

        lax.fori_loop(0, 4, tile, 0)

    def up32(value):
        return value.astype(F32)

    def ring_reduce(view, landing, width):
        half = width // 2
        lo, hi = pl.ds(0, half), pl.ds(half, half)
        right = send(view(z + 4, lo), landing(0, 0, lo), at(az=1))
        left = send(view(z + 4, hi), landing(1, 0, hi), at(az=-1))
        yield
        full = pl.ds(0, width)
        for step in (1, 2, 3):
            cols = lo if step == 1 else full
            right.wait_recv()
            mine = view(z + 4 - step, cols)
            mine[...] = (up32(mine[...]) + up32(landing(0, step - 1, cols)[...])).astype(BF16)
            mine = view(z + 4 - step, full)
            next_right = send(mine, landing(0, step, full), at(az=1))
            cols = hi if step == 1 else full
            left.wait_recv()
            mine = view(z - 4 + step, cols)
            mine[...] = (up32(mine[...]) + up32(landing(1, step - 1, cols)[...])).astype(BF16)
            mine = view(z - 4 + step, full)
            next_left = send(mine, landing(1, step, full), at(az=-1))
            right, left = next_right, next_left
            yield
        right.wait_recv()
        left.wait_recv()

    def reduce_wide_z(j):
        yield from ring_reduce(
            lambda zz, cols: o.at[j, slot(zz), :, :, cols],
            lambda way, step, cols: zl.at[j, way, step, :, :, cols],
            1024,
        )
        mine = o.at[j, slot(z)]
        mine[...] = (up32(mine[...]) + up32(zl[j, 0, 3]) + up32(zl[j, 1, 3])).astype(BF16)
        sends = [send(mine.at[lax.rem(x + i, 4)], xl.at[j, i - 1], at(ax=i)) for i in (1, 3, 2)]
        yield
        for copy in sends:
            copy.wait_recv()
        total = up32(mine[x]) + up32(xl[j, 0]) + up32(xl[j, 1]) + up32(xl[j, 2])
        out_ref[j * S:(j + 1) * S, :] = total.astype(BF16)

    def reduce_wide_x(j):
        lo, hi = pl.ds(0, 512), pl.ds(512, 512)
        right_x, left_x, far_x = lax.rem(x + 1, 4), lax.rem(x + 3, 4), lax.rem(x + 2, 4)
        right = send(o.at[j, :, far_x, :, lo], xd.at[j, 0], at(ax=1))
        left = send(o.at[j, :, far_x, :, hi], xd.at[j, 1], at(ax=-1))
        plain_right = send(o.at[j, :, right_x, :, hi], xf.at[j, 0], at(ax=1))
        plain_left = send(o.at[j, :, left_x, :, lo], xf.at[j, 1], at(ax=-1))
        yield
        right.wait_recv()
        o[j, :, right_x, :, lo] = (up32(o[j, :, right_x, :, lo]) + up32(xd[j, 0])).astype(BF16)
        right = send(o.at[j, :, right_x, :, lo], xf.at[j, 2], at(ax=1))
        left.wait_recv()
        o[j, :, left_x, :, hi] = (up32(o[j, :, left_x, :, hi]) + up32(xd[j, 1])).astype(BF16)
        left = send(o.at[j, :, left_x, :, hi], xf.at[j, 3], at(ax=-1))
        yield
        plain_right.wait_recv()
        plain_left.wait_recv()
        right.wait_recv()
        left.wait_recv()
        zb[j, 0, :, :, lo] = (up32(o[j, :, x, :, lo]) + up32(xf[j, 1]) + up32(xf[j, 2])).astype(BF16)
        zb[j, 0, :, :, hi] = (up32(o[j, :, x, :, hi]) + up32(xf[j, 0]) + up32(xf[j, 3])).astype(BF16)
        yield from ring_reduce(
            lambda zz, cols: zb.at[j, 0, slot(zz), :, cols],
            lambda way, step, cols: zl.at[j, way, step, 0, :, cols],
            1024,
        )
        total = up32(zb[j, 0, slot(z)]) + up32(zl[j, 0, 3, 0]) + up32(zl[j, 1, 3, 0])
        out_ref[j * S:(j + 1) * S, :] = total.astype(BF16)

    def part(j):
        arrive(j)
        yield from (gather_wide_z if j % 2 == 0 else gather_wide_x)(j)
        if j == 0:
            loads[0].wait()
            loads[1].wait()
        gate_up(j, 1 - k)
        pair = send(g.at[j, pl.ds((1 - k) * 4, 4)], pr.at[j], partner)
        gate_up(j, k)
        yield
        pair.wait_recv()
        ahead, behind, far = lax.rem(y + 1, 4), lax.rem(y + 3, 4), lax.rem(y + 2, 4)

        def add_pair(yy):
            g[j, k * 4 + yy] = (up32(g[j, k * 4 + yy]) + up32(pr[j, yy])).astype(BF16)

        lo, hi = pl.ds(0, 896), pl.ds(896, 896)
        add_pair(far)
        right = send(g.at[j, k * 4 + far, :, lo], yl.at[j, 0], at(ay=1))
        left = send(g.at[j, k * 4 + far, :, hi], yl.at[j, 1], at(ay=-1))
        add_pair(ahead)
        plain_right = send(g.at[j, k * 4 + ahead, :, hi], yf.at[j, 0], at(ay=1))
        add_pair(behind)
        plain_left = send(g.at[j, k * 4 + behind, :, lo], yf.at[j, 1], at(ay=-1))
        add_pair(y)
        yield
        right.wait_recv()
        comb[j, 0] = (up32(g[j, k * 4 + ahead, :, lo]) + up32(yl[j, 0])).astype(BF16)
        right = send(comb.at[j, 0], yf.at[j, 2], at(ay=1))
        left.wait_recv()
        comb[j, 1] = (up32(g[j, k * 4 + behind, :, hi]) + up32(yl[j, 1])).astype(BF16)
        left = send(comb.at[j, 1], yf.at[j, 3], at(ay=-1))
        yield
        plain_right.wait_recv()
        plain_left.wait_recv()
        right.wait_recv()
        left.wait_recv()
        factor = fb[:, j * S:(j + 1) * S, :].reshape(M, 128)[:, 0:1]
        gate = (up32(g[j, k * 4 + y, :, lo]) + up32(yf[j, 1]) + up32(yf[j, 2])) * factor
        up = (up32(g[j, k * 4 + y, :, hi]) + up32(yf[j, 0]) + up32(yf[j, 3])) * factor
        h[j, k * 4 + y] = (gate / (1.0 + jnp.exp(-gate)) * up).astype(BF16)
        block = h.at[j, k * 4 + y]
        right = send(block, block, at(ay=1))
        left = send(block, block, at(ay=-1))
        pairs = [send(block, block, partner)]
        yield
        right.wait_recv()
        src = h.at[j, k * 4 + behind, pl.ds(0, M // 2)]
        next_right = send(src, src, at(ay=1))
        left.wait_recv()
        src = h.at[j, k * 4 + ahead, pl.ds(M // 2, M // 2)]
        next_left = send(src, src, at(ay=-1))
        for yy in (behind, ahead):
            block = h.at[j, k * 4 + yy]
            pairs.append(send(block, block, partner))
        yield
        next_right.wait_recv()
        next_left.wait_recv()
        block = h.at[j, k * 4 + far]
        pairs.append(send(block, block, partner))
        if j == 0:
            loads[2].wait()
        down(j, k)
        for copy in pairs:
            copy.wait_recv()
        down(j, 1 - k)
        yield from (reduce_wide_x if j % 2 == 0 else reduce_wide_z)(j)

    running = [(0, norm())] + [(LAG * j, part(j)) for j in range(PARTS)]
    stage = 0
    while running:
        left_over = []
        for begin, work in running:
            if stage < begin or next(work, "end") != "end":
                left_over.append((begin, work))
        running = left_over
        stage += 1

    @pl.when(jnp.logical_not(stays))
    def _():
        for move in moves:
            move.wait_send()

    for copy in started:
        copy.wait_send()


def local(tokens, norm_gain, gate_weight, up_weight, down_weight):
    vmem = pl.BlockSpec(memory_space=pltpu.VMEM)
    hbm = pl.BlockSpec(memory_space=pl.ANY)
    K = PARTS
    return pl.pallas_call(
        kernel,
        out_shape=jax.ShapeDtypeStruct((64, 1024), BF16),
        in_specs=[vmem, vmem, hbm, hbm, hbm],
        out_specs=vmem,
        scratch_shapes=[
            pltpu.VMEM((1024, 1792), BF16),
            pltpu.VMEM((896, 1024), BF16),
            pltpu.VMEM((K, M, 256), BF16),
            pltpu.VMEM((K, 8, M, 1024), BF16),
            pltpu.VMEM((K, 8, M, 1792), BF16),
            pltpu.VMEM((K, 4, M, 1792), BF16),
            pltpu.VMEM((K, 2, M, 896), BF16),
            pltpu.VMEM((K, 4, M, 896), BF16),
            pltpu.VMEM((K, 2, M, 896), BF16),
            pltpu.VMEM((K, 8, M, 896), BF16),
            pltpu.VMEM((K, 8, 4, S, 1024), BF16),
            pltpu.VMEM((K, 2, 4, 4, S, 1024), BF16),
            pltpu.VMEM((K, 3, S, 1024), BF16),
            pltpu.VMEM((K, 2, 8, S, 512), BF16),
            pltpu.VMEM((K, 4, 8, S, 512), BF16),
            pltpu.VMEM((K, 1, 8, S, 1024), BF16),
            pltpu.VMEM((2, 8, 256), F32),
            pltpu.VMEM((3, 8, 256), F32),
            pltpu.VMEM((7, 8, 256), F32),
            pltpu.VMEM((4, 64, 128), F32),
            pltpu.SemaphoreType.DMA((3,)),
            pltpu.SemaphoreType.DMA((COPIES,)),
            pltpu.SemaphoreType.DMA((COPIES,)),
        ],
        compiler_params=pltpu.CompilerParams(
            collective_id=0, has_side_effects=True, vmem_limit_bytes=58 * 2**20
        ),
        cost_estimate=pl.CostEstimate(flops=11_300_000_000, bytes_accessed=6_000_000, transcendentals=230_000),
        name="swiglu_block",
    )(tokens.reshape(4, 64, 256), norm_gain.reshape(32, 256), gate_weight, up_weight, down_weight)


def solution(mesh):
    return jax.shard_map(
        local,
        mesh=mesh,
        in_specs=(P("row", "col"), P(), P("row", "col"), P("row", "col"), P("col", "row")),
        out_specs=P("col", "row"),
        check_vma=False,
    )
```

time: 569 us -> 174 us (0.31)
  waiting for transfers between devices: 388 us -> 0 us
  Pallas kernels: 0 us -> 169 us
  blocking collectives: 121 us -> 0 us
  matrix products: 22.6 us -> 0 us
  between operations: 13.2 us -> 0.01 us
  other arithmetic: 10.7 us -> 0 us
    reduce_scatter x2 -> x0, waiting for transfers between devices: 262 us -> none  [the longest x1 217 us: local(): lax.psum_scatter(partial_value.astype(jnp.bfloat16), 'col', scatter_dimen...]
    pallas_call x0 -> x1, Pallas kernels: none -> 169 us  [local(): pl.pallas_call(kernel, out_shape=jax.ShapeDtypeStruct((64, 1024), BF16),...]
    all_gather x2 -> x0, waiting for transfers between devices: 125 us -> none  [the longest x1 88.2 us: local(): features = lax.all_gather(normed, 'col', axis=1, tiled=True)]
    psum x1 -> x0, blocking collectives: 64.3 us -> none  [local(): squares = lax.psum(jnp.sum(values * values, axis=1), 'col')]
    all_to_all x1 -> x0, blocking collectives: 57.1 us -> none  [local(): lax.all_to_all(features, 'row', split_axis=1, concat_axis=0, tiled=True)]
    dot_general x3 -> x0, matrix products: 22.6 us -> none  [the longest x1 8.83 us: local(): up_term = jnp.dot(columns, up_weight, preferred_element_type=jnp.float32)]
    concatenate x1 -> x0, other arithmetic: 7.5 us -> none  [local(): jnp.concatenate([gate_term, up_term], axis=1).astype(jnp.bfloat16)]
    all_to_all x1 -> x0, local copies, waits for them, and re-layouts: 6.49 us -> none  [local(): lax.all_to_all(features, 'row', split_axis=1, concat_axis=0, tiled=True)]
  transfers between devices with their start and end apart: 4 -> 0, of which waited for: 4 -> 0; matrix products, arithmetic and copies ran while one was open for 0% -> 0% of each run, Pallas kernels for 0% -> 0%
where the time goes in v1:
time: 174 us; the launch traced here: 172 us
  Pallas kernels  169 us (97%)
  local copies, waits for them, and re-layouts  2.95 us (2%)
    pallas_call x1, Pallas kernels, local(): pl.pallas_call(kernel, out_shape=jax.ShapeDtypeStruct((64, 1024), BF16),...  169 us

profile of v1, /device:TPU:1, one launch (start us, length us, event | category | flops | bytes accessed | tf_op | source)
XLA Modules:
  0.0 171.6 jit_solution(1699138121998031766)
XLA Ops:
  0.0 1.4 reshape.7.gain_ref
  1.4 168.7 %swiglu_block.1 = bf16[64,1024]{1,0:T(8,128)(2,1)} custom-call(bf16[4,64,256]{2,1,0:T(8,128)(2,1)} %bitcast.1, f32[32,256]{1,0:T(8,128)} %reshape.7.gain_ref, bf16[1024,896]{1,0:T(8,128)(2,1)} %gate_hbm.1, bf16[1024,896]{1,0:T(8,128)(2,1)} %up_hbm.1, bf16[896,1024]{1,0:T(8,128)(2,1)} %down_hbm.1), custom_call_target="tpu_custom_call" | custom-call | flops 11299999744 | bytes 6000000 | tf_op jit(solution)/shard_map/swiglu_block/pallas_call | solution.py:376
  170.0 1.6 copy.7

commit v2 on v0

v2 whole, which is shorter than its diff:
```python
import jax
import jax.numpy as jnp
from jax import lax
from jax.experimental import pallas as pl
from jax.experimental.pallas import tpu as pltpu
from jax.sharding import PartitionSpec as P

D = 8192
EPSILON = 1e-05
BF16 = jnp.bfloat16
F32 = jnp.float32
MESH = pl.DeviceIdType.MESH

WAVES = ((0, 1), (1, 2), (3, 2), (5, 2), (7, 1))
START = (0.0, 14.0, 25.0, 37.0, 43.0)
STAGE = (4.0, 4.5, 4.5, 4.5, 4.5)
COPIES = 150


def kernel(
    tok_ref, gain_ref, gate_hbm, up_hbm, down_hbm, out_ref,
    w, wd, st, xs, g, pr, yl, yf, comb, h, o, xd, xf, zb, zl, ss, sx, sz, fa,
    wsem, send_sems, recv_sems,
):
    row = lax.axis_index("row")
    col = lax.axis_index("col")
    y, k = lax.div(row, 2), lax.rem(row, 2)
    z, x = lax.div(col, 4), lax.rem(col, 4)
    ahead, behind, far = lax.rem(y + 1, 4), lax.rem(y + 3, 4), lax.rem(y + 2, 4)
    right_x, left_x, far_x = lax.rem(x + 1, 4), lax.rem(x + 3, 4), lax.rem(x + 2, 4)

    def at(ax=0, ay=0, az=0):
        yy = lax.rem(y + ay + 4, 4)
        zz = lax.rem(z + az + 8, 8)
        xx = lax.rem(x + ax + 4, 4)
        return (2 * yy + k, 4 * zz + xx)

    partner = (2 * y + 1 - k, col)
    rows = [(lax.rem(row + i, 8), col) for i in range(1, 8)]
    perm_target = (z, 4 * lax.rem(row + 4, 8) + x)
    perm_source = (lax.rem(z + 4, 8), 4 * row + x)

    barrier = pltpu.get_barrier_semaphore()
    others = [at(ax=i) for i in (1, 2, 3)] + [at(az=i) for i in range(1, 8)] + rows + [perm_source]
    for device in others:
        pl.semaphore_signal(barrier, inc=1, device_id=device, device_id_type=MESH)

    loads = [
        pltpu.make_async_copy(gate_hbm, w.at[:, 0:896], wsem.at[0]),
        pltpu.make_async_copy(up_hbm, w.at[:, 896:1792], wsem.at[1]),
        pltpu.make_async_copy(down_hbm, wd, wsem.at[2]),
    ]
    for load in loads:
        load.start()

    started = []

    def send(src, dst, device):
        index = len(started)
        copy = pltpu.make_async_remote_copy(
            src_ref=src, dst_ref=dst,
            send_sem=send_sems.at[index], recv_sem=recv_sems.at[index],
            device_id=device, device_id_type=MESH,
        )
        copy.start()
        started.append(copy)
        return copy

    def up32(value):
        return value.astype(F32)

    values = up32(tok_ref[...])
    st[...] = (values * gain_ref[pl.ds(col, 1), :]).astype(BF16)
    squares = jnp.sum(values * values, axis=1, keepdims=True)
    diagonal = lax.broadcasted_iota(jnp.int32, (256, 256), 0) == lax.broadcasted_iota(jnp.int32, (256, 256), 1)
    ss[0] = jnp.broadcast_to(jnp.sum(jnp.where(diagonal, squares, 0.0), axis=0, keepdims=True), (8, 256))

    pl.semaphore_wait(barrier, len(others))

    mine = pl.ds(pl.multiple_of(x * 256, 256), 256)
    move = send(st, xs.at[0, :, mine], perm_target)

    def norm():
        sends = [send(ss.at[0], sx.at[i - 1], at(ax=i)) for i in (1, 2, 3)]
        yield
        for copy in sends:
            copy.wait_recv()
        ss[1] = ss[0] + sx[0] + sx[1] + sx[2]
        sends = [send(ss.at[1], sz.at[i - 1], at(az=i)) for i in range(1, 8)]
        yield
        for copy in sends:
            copy.wait_recv()
        total = ss[1]
        for i in range(7):
            total = total + sz[i]
        fa[row] = lax.rsqrt(total / D + EPSILON)
        sends = [send(fa.at[row], fa.at[row], device) for device in rows]
        yield
        for copy in sends:
            copy.wait_recv()

    arrivals = {}

    def stream():
        move.wait_recv()
        block = xs.at[0, :, mine]
        sends = [send(block, block, at(ax=i)) for i in (1, 3, 2)]
        yield
        for copy in sends:
            copy.wait_recv()
        arrivals[0] = []
        pair = [send(xs.at[0], xs.at[1], at(az=1)), send(xs.at[0], xs.at[2], at(az=-1))]
        for wave in (1, 2, 3):
            yield
            a, b = 2 * wave - 1, 2 * wave
            lo, hi = (pl.ds(0, 128), pl.ds(128, 128)) if wave == 3 else (pl.ds(0, 256), pl.ds(0, 256))
            to_a, to_b = (7, 7) if wave == 3 else (a + 2, b + 2)
            pair[0].wait_recv()
            next_a = send(xs.at[a, lo], xs.at[to_a, lo], at(az=1))
            pair[1].wait_recv()
            next_b = send(xs.at[b, hi], xs.at[to_b, hi], at(az=-1))
            pair = [next_a, next_b]
            arrivals[wave] = []
        arrivals[4] = pair

    def gate_up(blocks, n, half):
        def tile(i, carry):
            cols = pl.ds(pl.multiple_of(i * 256, 256), 256)
            left = xs[blocks, pl.ds(half * 128, 128), :].reshape(n * 128, 1024)
            result = jnp.dot(left, w[:, cols], preferred_element_type=F32)
            g[blocks, half, :, :, cols] = result.astype(BF16).reshape(n, 4, 32, 256)
            return carry

        lax.fori_loop(0, 7, tile, 0)

    def down(blocks, n, half):
        def tile(i, carry):
            cols = pl.ds(pl.multiple_of(i * 256, 256), 256)
            left = h[blocks, half].reshape(n * 128, 896)
            result = jnp.dot(left, wd[:, cols], preferred_element_type=F32)
            o[blocks, pl.ds(half * 2, 2), :, cols] = result.astype(BF16).reshape(n, 2, 64, 256)
            return carry

        lax.fori_loop(0, 4, tile, 0)

    def factors(block):
        if block == 0:
            t = lax.rem(z + 4, 8)
        elif block == 7:
            t = z
        elif block % 2:
            t = lax.rem(z + 12 - (block + 1) // 2, 8)
        else:
            t = lax.rem(z + 4 + block // 2, 8)
        token = lax.broadcasted_iota(jnp.int32, (32, 256), 0) + (k * 128 + y * 32)
        lane = lax.broadcasted_iota(jnp.int32, (32, 256), 1)
        return jnp.sum(jnp.where(token == lane, fa[t, 0:1, :], 0.0), axis=1, keepdims=True)

    chain = {}

    def work(index):
        first, n = WAVES[index]
        blocks = pl.ds(first, n)
        for copy in arrivals[index]:
            copy.wait_recv()
        if index == 0:
            loads[0].wait()
            loads[1].wait()
        gate_up(blocks, n, 1 - k)
        pair = send(g.at[blocks, 1 - k], pr.at[blocks], partner)
        gate_up(blocks, n, k)
        yield
        pair.wait_recv()

        def add_pair(yy):
            g[blocks, k, yy] = (up32(g[blocks, k, yy]) + up32(pr[blocks, yy])).astype(BF16)

        lo, hi = pl.ds(0, 896), pl.ds(896, 896)
        add_pair(far)
        right = send(g.at[blocks, k, far, :, lo], yl.at[0, blocks], at(ay=1))
        left = send(g.at[blocks, k, far, :, hi], yl.at[1, blocks], at(ay=-1))
        add_pair(ahead)
        plain_right = send(g.at[blocks, k, ahead, :, hi], yf.at[0, blocks], at(ay=1))
        add_pair(behind)
        plain_left = send(g.at[blocks, k, behind, :, lo], yf.at[1, blocks], at(ay=-1))
        add_pair(y)
        yield
        right.wait_recv()
        comb[0, blocks] = (up32(g[blocks, k, ahead, :, lo]) + up32(yl[0, blocks])).astype(BF16)
        right = send(comb.at[0, blocks], yf.at[2, blocks], at(ay=1))
        left.wait_recv()
        comb[1, blocks] = (up32(g[blocks, k, behind, :, hi]) + up32(yl[1, blocks])).astype(BF16)
        left = send(comb.at[1, blocks], yf.at[3, blocks], at(ay=-1))
        yield
        for copy in (plain_right, plain_left, right, left):
            copy.wait_recv()
        for block in range(first, first + n):
            factor = factors(block)
            gate = (up32(g[block, k, y, :, lo]) + up32(yf[1, block]) + up32(yf[2, block])) * factor
            up = (up32(g[block, k, y, :, hi]) + up32(yf[0, block]) + up32(yf[3, block])) * factor
            h[block, k, y] = (gate / (1.0 + jnp.exp(-gate)) * up).astype(BF16)
        view = h.at[blocks, k, y]
        right = send(view, view, at(ay=1))
        left = send(view, view, at(ay=-1))
        pairs = [send(view, view, partner)]
        yield
        right.wait_recv()
        view = h.at[blocks, k, behind, pl.ds(0, 16)]
        next_right = send(view, view, at(ay=1))
        left.wait_recv()
        view = h.at[blocks, k, ahead, pl.ds(16, 16)]
        next_left = send(view, view, at(ay=-1))
        for yy in (behind, ahead):
            view = h.at[blocks, k, yy]
            pairs.append(send(view, view, partner))
        yield
        next_right.wait_recv()
        next_left.wait_recv()
        view = h.at[blocks, k, far]
        pairs.append(send(view, view, partner))
        if index == 0:
            loads[2].wait()
        down(blocks, n, k)
        yield
        for copy in pairs:
            copy.wait_recv()
        down(blocks, n, 1 - k)
        lo, hi = pl.ds(0, 512), pl.ds(512, 512)
        right = send(o.at[blocks, far_x, :, lo], xd.at[0, blocks], at(ax=1))
        left = send(o.at[blocks, far_x, :, hi], xd.at[1, blocks], at(ax=-1))
        plain_right = send(o.at[blocks, right_x, :, hi], xf.at[0, blocks], at(ax=1))
        plain_left = send(o.at[blocks, left_x, :, lo], xf.at[1, blocks], at(ax=-1))
        yield
        right.wait_recv()
        o[blocks, right_x, :, lo] = (up32(o[blocks, right_x, :, lo]) + up32(xd[0, blocks])).astype(BF16)
        right = send(o.at[blocks, right_x, :, lo], xf.at[2, blocks], at(ax=1))
        left.wait_recv()
        o[blocks, left_x, :, hi] = (up32(o[blocks, left_x, :, hi]) + up32(xd[1, blocks])).astype(BF16)
        left = send(o.at[blocks, left_x, :, hi], xf.at[3, blocks], at(ax=-1))
        yield
        for copy in (plain_right, plain_left, right, left):
            copy.wait_recv()
        for block in range(first, first + n):
            low = up32(o[block, x, :, lo]) + up32(xf[1, block]) + up32(xf[2, block])
            high = up32(o[block, x, :, hi]) + up32(xf[0, block]) + up32(xf[3, block])
            if index in (1, 2, 3):
                way = (block + 1) % 2
                chain[way].wait_recv()
                if index > 1 or way == 0:
                    low = low + up32(zl[way, index - 1, :, lo])
                if index > 1 or way == 1:
                    high = high + up32(zl[way, index - 1, :, hi])
            if index == 4:
                for way in (0, 1):
                    chain[way].wait_recv()
                    low = low + up32(zl[way, 3, :, lo])
                    high = high + up32(zl[way, 3, :, hi])
                out_ref[:, lo] = low.astype(BF16)
                out_ref[:, hi] = high.astype(BF16)
                continue
            zb[block, :, lo] = low.astype(BF16)
            zb[block, :, hi] = high.astype(BF16)
            if index == 0:
                chain[0] = send(zb.at[0, :, lo], zl.at[0, 0, :, lo], at(az=1))
                chain[1] = send(zb.at[0, :, hi], zl.at[1, 0, :, hi], at(az=-1))
            else:
                chain[way] = send(zb.at[block], zl.at[way, index], at(az=1 if way == 0 else -1))

    steps = []
    for i, when in enumerate((-9.0, -0.5, START[1] - 0.5, START[2] - 0.5, START[3] - 0.5)):
        steps.append((when, 0, "stream"))
    for i, when in enumerate((-10.0, -5.0, 2.0, START[0] + 2.5 * STAGE[0])):
        steps.append((when, 1, "norm"))
    for index in range(5):
        for stage in range(9):
            steps.append((START[index] + stage * STAGE[index], 2 + index, index))
    running = {"stream": stream(), "norm": norm()}
    running.update({index: work(index) for index in range(5)})
    for _, _, name in sorted(steps, key=lambda s: (s[0], s[1])):
        next(running[name], None)

    for copy in started:
        copy.wait_send()


def local(tokens, norm_gain, gate_weight, up_weight, down_weight):
    vmem = pl.BlockSpec(memory_space=pltpu.VMEM)
    hbm = pl.BlockSpec(memory_space=pl.ANY)
    return pl.pallas_call(
        kernel,
        out_shape=jax.ShapeDtypeStruct((64, 1024), BF16),
        in_specs=[vmem, vmem, hbm, hbm, hbm],
        out_specs=vmem,
        scratch_shapes=[
            pltpu.VMEM((1024, 1792), BF16),
            pltpu.VMEM((896, 1024), BF16),
            pltpu.VMEM((256, 256), BF16),
            pltpu.VMEM((8, 256, 1024), BF16),
            pltpu.VMEM((8, 2, 4, 32, 1792), BF16),
            pltpu.VMEM((8, 4, 32, 1792), BF16),
            pltpu.VMEM((2, 8, 32, 896), BF16),
            pltpu.VMEM((4, 8, 32, 896), BF16),
            pltpu.VMEM((2, 8, 32, 896), BF16),
            pltpu.VMEM((8, 2, 4, 32, 896), BF16),
            pltpu.VMEM((8, 4, 64, 1024), BF16),
            pltpu.VMEM((2, 8, 64, 512), BF16),
            pltpu.VMEM((4, 8, 64, 512), BF16),
            pltpu.VMEM((8, 64, 1024), BF16),
            pltpu.VMEM((2, 4, 64, 1024), BF16),
            pltpu.VMEM((2, 8, 256), F32),
            pltpu.VMEM((3, 8, 256), F32),
            pltpu.VMEM((7, 8, 256), F32),
            pltpu.VMEM((8, 8, 256), F32),
            pltpu.SemaphoreType.DMA((3,)),
            pltpu.SemaphoreType.DMA((COPIES,)),
            pltpu.SemaphoreType.DMA((COPIES,)),
        ],
        compiler_params=pltpu.CompilerParams(
            collective_id=0, has_side_effects=True, vmem_limit_bytes=58 * 2**20
        ),
        cost_estimate=pl.CostEstimate(flops=11_300_000_000, bytes_accessed=6_000_000, transcendentals=230_000),
        name="swiglu_block",
    )(tokens, norm_gain.reshape(32, 256), gate_weight, up_weight, down_weight)


def solution(mesh):
    return jax.shard_map(
        local,
        mesh=mesh,
        in_specs=(P("row", "col"), P(), P("row", "col"), P("row", "col"), P("col", "row")),
        out_specs=P("col", "row"),
        check_vma=False,
    )
```

time: 569 us -> 124 us (0.22)
  waiting for transfers between devices: 388 us -> 0 us
  blocking collectives: 121 us -> 0 us
  Pallas kernels: 0 us -> 119 us
  matrix products: 22.6 us -> 0 us
  between operations: 13.2 us -> 0.01 us
  other arithmetic: 10.7 us -> 0 us
    reduce_scatter x2 -> x0, waiting for transfers between devices: 262 us -> none  [the longest x1 217 us: local(): lax.psum_scatter(partial_value.astype(jnp.bfloat16), 'col', scatter_dimen...]
    all_gather x2 -> x0, waiting for transfers between devices: 125 us -> none  [the longest x1 88.2 us: local(): features = lax.all_gather(normed, 'col', axis=1, tiled=True)]
    pallas_call x0 -> x1, Pallas kernels: none -> 119 us  [local(): pl.pallas_call(kernel, out_shape=jax.ShapeDtypeStruct((64, 1024), BF16),...]
    psum x1 -> x0, blocking collectives: 64.3 us -> none  [local(): squares = lax.psum(jnp.sum(values * values, axis=1), 'col')]
    all_to_all x1 -> x0, blocking collectives: 57.1 us -> none  [local(): lax.all_to_all(features, 'row', split_axis=1, concat_axis=0, tiled=True)]
    dot_general x3 -> x0, matrix products: 22.6 us -> none  [the longest x1 8.83 us: local(): up_term = jnp.dot(columns, up_weight, preferred_element_type=jnp.float32)]
    concatenate x1 -> x0, other arithmetic: 7.5 us -> none  [local(): jnp.concatenate([gate_term, up_term], axis=1).astype(jnp.bfloat16)]
    all_to_all x1 -> x0, local copies, waits for them, and re-layouts: 6.49 us -> none  [local(): lax.all_to_all(features, 'row', split_axis=1, concat_axis=0, tiled=True)]
  transfers between devices with their start and end apart: 4 -> 0, of which waited for: 4 -> 0; matrix products, arithmetic and copies ran while one was open for 0% -> 0% of each run, Pallas kernels for 0% -> 0%
where the time goes in v2:
time: 124 us; the launch traced here: 122 us
  Pallas kernels  119 us (96%)
  local copies, waits for them, and re-layouts  2.95 us (2%)
    pallas_call x1, Pallas kernels, local(): pl.pallas_call(kernel, out_shape=jax.ShapeDtypeStruct((64, 1024), BF16),...  119 us

profile of v2, /device:TPU:1, one launch (start us, length us, event | category | flops | bytes accessed | tf_op | source)
XLA Modules:
  0.0 122.0 jit_solution(3416989263302253157)
XLA Ops:
  0.0 1.4 %reshape.3.gain_ref = f32[32,256]{1,0:T(8,128)} reshape(f32[8192]{0:T(1024)} %param.6) | data formatting | bytes 65536 | tf_op jit(solution)/shard_map/reshape | solution.py:323
  1.4 119.0 %swiglu_block.1 = bf16[64,1024]{1,0:T(8,128)(2,1)} custom-call(bf16[256,256]{1,0:T(8,128)(2,1)} %tok_ref.1, f32[32,256]{1,0:T(8,128)} %reshape.3.gain_ref, bf16[1024,896]{1,0:T(8,128)(2,1)} %gate_hbm.1, bf16[1024,896]{1,0:T(8,128)(2,1)} %up_hbm.1, bf16[896,1024]{1,0:T(8,128)(2,1)} %down_hbm.1), custom_call_target="tpu_custom_call" | custom-call | flops 11299999744 | bytes 6000000 | tf_op jit(solution)/shard_map/swiglu_block/pallas_call | solution.py:289
  120.4 1.6 %copy.7 = bf16[64,1024]{1,0:T(8,128)(2,1)} copy(bf16[64,1024]{1,0:T(8,128)(2,1)} %swiglu_block.1) | data formatting | bytes 262144

commit v3 on v2

v3 whole, which is shorter than its diff:
```python
import jax
import jax.numpy as jnp
from jax import lax
from jax.experimental import pallas as pl
from jax.experimental.pallas import tpu as pltpu
from jax.sharding import PartitionSpec as P

D = 8192
EPSILON = 1e-05
BF16 = jnp.bfloat16
F32 = jnp.float32
MESH = pl.DeviceIdType.MESH

GROUPS = (
    (0, 0, 1),
    (1, 1, 1),
    (1, 2, 1),
    (2, 3, 1),
    (2, 4, 1),
    (3, 5, 1),
    (3, 6, 1),
    (4, 7, 1),
)

ORDER = (
    9, 8, 9, 8, 0, 9, 0, 9, 8, 1, 0, 2, 9, 1, 2, 9, 8, 0, 9, 1, 2, 3, 4, 0,
    3, 8, 1, 9, 0, 2, 3, 4, 9, 0, 1, 5, 2, 9, 3, 4, 0, 5, 6, 1, 2, 3, 0, 1,
    2, 4, 7, 5, 6, 3, 1, 4, 3, 5, 2, 6, 7, 4, 1, 5, 4, 6, 3, 7, 2, 5, 4, 6,
    5, 7, 3, 6, 4, 6, 5, 7, 7, 6, 7, 5, 6, 7, 7,
)
COPIES = 260
POOL = 48
WIDE = 96


def kernel(
    tok_ref, gain_ref, gate_hbm, up_hbm, down_hbm, out_ref,
    w, wd, st, xs, g, pr, yl, yf, comb, h, o, xd, xf, zb, zl, ss, sx, sy, fa,
    wsem, send_sems, recv_sems,
):
    row = lax.axis_index("row")
    col = lax.axis_index("col")
    y, k = lax.div(row, 2), lax.rem(row, 2)
    z, x = lax.div(col, 4), lax.rem(col, 4)
    ahead, behind, far = lax.rem(y + 1, 4), lax.rem(y + 3, 4), lax.rem(y + 2, 4)
    right_x, left_x, far_x = lax.rem(x + 1, 4), lax.rem(x + 3, 4), lax.rem(x + 2, 4)

    def at(ax=0, ay=0, az=0):
        yy = lax.rem(y + ay + 4, 4)
        zz = lax.rem(z + az + 8, 8)
        xx = lax.rem(x + ax + 4, 4)
        return (2 * yy + k, 4 * zz + xx)

    partner = (2 * y + 1 - k, col)
    perm_target = (z, 4 * lax.rem(row + 4, 8) + x)
    perm_source = (lax.rem(z + 4, 8), 4 * row + x)

    barrier = pltpu.get_barrier_semaphore()
    others = [perm_source, at(az=1), at(az=-1), at(ax=1), at(ax=2), at(ax=3), at(ay=1), at(ay=-1), partner]
    for device in others:
        pl.semaphore_signal(barrier, inc=1, device_id=device, device_id_type=MESH)

    loads = [
        pltpu.make_async_copy(gate_hbm, w.at[:, 0:896], wsem.at[0]),
        pltpu.make_async_copy(up_hbm, w.at[:, 896:1792], wsem.at[1]),
        pltpu.make_async_copy(down_hbm, wd, wsem.at[2]),
    ]
    for load in loads:
        load.start()

    started = []

    def send(src, dst, device):
        index = len(started)
        if index >= POOL:
            started[index - POOL].wait_send()
        copy = pltpu.make_async_remote_copy(
            src_ref=src, dst_ref=dst,
            send_sem=send_sems.at[index % POOL], recv_sem=recv_sems.at[index],
            device_id=device, device_id_type=MESH,
        )
        copy.start()
        started.append(copy)
        return copy

    def up32(value):
        return value.astype(F32)

    values = up32(tok_ref[...])
    st[...] = (values * gain_ref[pl.ds(pl.multiple_of(col * 256, 256), 256)].reshape(1, 256)).astype(BF16)
    squares = jnp.sum(values * values, axis=1, keepdims=True)
    diagonal = lax.broadcasted_iota(jnp.int32, (256, 256), 0) == lax.broadcasted_iota(jnp.int32, (256, 256), 1)
    ss[0] = jnp.broadcast_to(jnp.sum(jnp.where(diagonal, squares, 0.0), axis=0, keepdims=True), (8, 256))

    pl.semaphore_wait(barrier, len(others))

    mine = pl.ds(pl.multiple_of(x * 256, 256), 256)
    moves = [
        send(st.at[part], xs.at[0, part, mine], perm_target)
        for part in (pl.ds(0, WIDE), pl.ds(WIDE, 256 - WIDE)) if part.size
    ]

    square_move = send(ss.at[0], ss.at[1], perm_target)

    def norm():
        yield
        square_move.wait_recv()
        sends = [send(ss.at[1], sx.at[i - 1], at(ax=i)) for i in (1, 2, 3)]
        yield
        for copy in sends:
            copy.wait_recv()
        ss[2] = ss[1] + sx[0] + sx[1] + sx[2]
        copy = send(ss.at[2], sy.at[3], partner)
        yield
        copy.wait_recv()
        ss[3] = ss[2] + sy[3]
        right, left = send(ss.at[3], sy.at[0], at(ay=1)), send(ss.at[3], sy.at[1], at(ay=-1))
        yield
        right.wait_recv()
        right = send(sy.at[0], sy.at[2], at(ay=1))
        left.wait_recv()
        yield
        right.wait_recv()
        fa[0] = lax.rsqrt((ss[3] + sy[0] + sy[1] + sy[2]) / D + EPSILON)
        right, left = send(fa.at[0], fa.at[1], at(az=1)), send(fa.at[0], fa.at[2], at(az=-1))
        for wave in (1, 2):
            yield
            right.wait_recv()
            right = send(fa.at[2 * wave - 1], fa.at[2 * wave + 1], at(az=1))
            left.wait_recv()
            left = send(fa.at[2 * wave], fa.at[2 * wave + 2], at(az=-1))
        yield
        right.wait_recv()
        right = send(fa.at[5], fa.at[7], at(az=1))
        left.wait_recv()
        yield
        right.wait_recv()

    arrivals = {}

    def stream():
        wide, narrow = pl.ds(0, WIDE), pl.ds(WIDE, 256 - WIDE)

        def over_x(blocks, part):
            view = xs.at[blocks, part, mine]
            return [send(view, view, at(ax=i)) for i in (1, 3, 2)]

        def halves(first, size):
            return pl.ds(first, size // 2), pl.ds(first + size // 2, size // 2)

        def forward(wave, part, cols):
            if wave == 0:
                source, target, rows_of = (0, 0), (1, 2), (part, part)
            elif wave < 3:
                source, target, rows_of = (2 * wave - 1, 2 * wave), (2 * wave + 1, 2 * wave + 2), (part, part)
            else:
                source, target, rows_of = (5, 6), (7, 7), halves(part.start, part.size)
            copies = []
            for way in (0, 1):
                if wave > 0:
                    ring[part.start][way].wait_recv()
                copies.append(send(
                    xs.at[source[way], rows_of[way], cols], xs.at[target[way], rows_of[way], cols],
                    at(az=1 - 2 * way)))
            ring[part.start] = copies

        everything = pl.ds(0, 1024)
        ring = {}
        for move in moves:
            move.wait_recv()
            if move is moves[0]:
                gathered = over_x(0, wide)
        if WIDE < 256:
            forward(0, narrow, mine)
            arrivals[0] = over_x(0, narrow)
        yield
        for copy in gathered:
            copy.wait_recv()
        forward(0, wide, everything)
        for wave in (1, 2, 3, 4):
            if WIDE < 256:
                if wave < 4:
                    forward(wave, narrow, mine)
                else:
                    for copy in ring[WIDE]:
                        copy.wait_recv()
                for group, (arrival, first, n) in enumerate(GROUPS):
                    if arrival == wave:
                        arrivals[group] = over_x(pl.ds(first, n), narrow)
            if wave < 4:
                yield
                forward(wave, wide, everything)
        arrivals[len(GROUPS) - 1] = arrivals.get(len(GROUPS) - 1, []) + ring[0]

    def gate_up(blocks, n, half, count):
        def tile(i, carry):
            cols = pl.ds(pl.multiple_of(i * 256, 256), 256)
            left = xs[blocks, pl.ds(half * 128, count * 128), :].reshape(n * count * 128, 1024)
            result = jnp.dot(left, w[:, cols], preferred_element_type=F32)
            g[blocks, pl.ds(half, count), :, :, cols] = result.astype(BF16).reshape(n, count, 4, 32, 256)
            return carry

        lax.fori_loop(0, 7, tile, 0, unroll=True)

    def down(blocks, n, half):
        def tile(i, carry):
            cols = pl.ds(pl.multiple_of(i * 256, 256), 256)
            left = h[blocks, half].reshape(n * 128, 896)
            result = jnp.dot(left, wd[:, cols], preferred_element_type=F32)
            o[blocks, pl.ds(half * 2, 2), :, cols] = result.astype(BF16).reshape(n, 2, 64, 256)
            return carry

        lax.fori_loop(0, 4, tile, 0, unroll=True)

    def factors(block):
        token = lax.broadcasted_iota(jnp.int32, (32, 256), 0) + (k * 128 + y * 32)
        lane = lax.broadcasted_iota(jnp.int32, (32, 256), 1)
        return jnp.sum(jnp.where(token == lane, fa[block, 0:1, :], 0.0), axis=1, keepdims=True)

    chain = {}

    def work(index):
        wave, first, n = GROUPS[index]
        blocks = pl.ds(first, n)
        for copy in arrivals.get(index, []):
            copy.wait_recv()
        if index == 0:
            loads[0].wait()
            loads[1].wait()
        gate_up(blocks, n, 1 - k, 1)
        pair = send(g.at[blocks, 1 - k], pr.at[blocks], partner)
        gate_up(blocks, n, k, 1)
        yield
        pair.wait_recv()

        def add_pair(yy):
            g[blocks, k, yy] = (up32(g[blocks, k, yy]) + up32(pr[blocks, yy])).astype(BF16)

        lo, hi = pl.ds(0, 896), pl.ds(896, 896)
        add_pair(far)
        right = send(g.at[blocks, k, far, :, lo], yl.at[0, blocks], at(ay=1))
        left = send(g.at[blocks, k, far, :, hi], yl.at[1, blocks], at(ay=-1))
        add_pair(ahead)
        plain_right = send(g.at[blocks, k, ahead, :, hi], yf.at[0, blocks], at(ay=1))
        add_pair(behind)
        plain_left = send(g.at[blocks, k, behind, :, lo], yf.at[1, blocks], at(ay=-1))
        add_pair(y)
        yield
        right.wait_recv()
        comb[0, blocks] = (up32(g[blocks, k, ahead, :, lo]) + up32(yl[0, blocks])).astype(BF16)
        right = send(comb.at[0, blocks], yf.at[2, blocks], at(ay=1))
        left.wait_recv()
        comb[1, blocks] = (up32(g[blocks, k, behind, :, hi]) + up32(yl[1, blocks])).astype(BF16)
        left = send(comb.at[1, blocks], yf.at[3, blocks], at(ay=-1))
        yield
        sums = [plain_right, plain_left, right, left]
        for copy in sums:
            copy.wait_recv()
        for block in range(first, first + n):
            factor = factors(block)
            gate, up = up32(g[block, k, y, :, lo]), up32(g[block, k, y, :, hi])
            gate = (gate + up32(yf[1, block]) + up32(yf[2, block])) * factor
            up = (up + up32(yf[0, block]) + up32(yf[3, block])) * factor
            h[block, k, y] = (gate / (1.0 + jnp.exp(-gate)) * up).astype(BF16)
        view = h.at[blocks, k, y]
        pairs = []

        def to_partner(*places):
            for yy in places:
                view = h.at[blocks, k, yy]
                pairs.append(send(view, view, partner))

        right = send(view, view, at(ay=1))
        left = send(view, view, at(ay=-1))
        to_partner(y)
        yield
        right.wait_recv()
        view = h.at[blocks, k, behind, pl.ds(0, 16)]
        next_right = send(view, view, at(ay=1))
        left.wait_recv()
        view = h.at[blocks, k, ahead, pl.ds(16, 16)]
        next_left = send(view, view, at(ay=-1))
        to_partner(behind, ahead)
        yield
        next_right.wait_recv()
        next_left.wait_recv()
        to_partner(far)
        if index == 0:
            loads[2].wait()
        down(blocks, n, k)
        yield
        for copy in pairs:
            copy.wait_recv()
        down(blocks, n, 1 - k)
        lo, hi = pl.ds(0, 512), pl.ds(512, 512)
        right = send(o.at[blocks, far_x, :, lo], xd.at[0, blocks], at(ax=1))
        left = send(o.at[blocks, far_x, :, hi], xd.at[1, blocks], at(ax=-1))
        plain_right = send(o.at[blocks, right_x, :, hi], xf.at[0, blocks], at(ax=1))
        plain_left = send(o.at[blocks, left_x, :, lo], xf.at[1, blocks], at(ax=-1))
        yield
        right.wait_recv()
        o[blocks, right_x, :, lo] = (up32(o[blocks, right_x, :, lo]) + up32(xd[0, blocks])).astype(BF16)
        right = send(o.at[blocks, right_x, :, lo], xf.at[2, blocks], at(ax=1))
        left.wait_recv()
        o[blocks, left_x, :, hi] = (up32(o[blocks, left_x, :, hi]) + up32(xd[1, blocks])).astype(BF16)
        left = send(o.at[blocks, left_x, :, hi], xf.at[3, blocks], at(ax=-1))
        yield
        sums = [plain_right, plain_left, right, left]
        for copy in sums:
            copy.wait_recv()
        for block in range(first, first + n):
            low, high = up32(o[block, x, :, lo]), up32(o[block, x, :, hi])
            low = low + up32(xf[1, block]) + up32(xf[2, block])
            high = high + up32(xf[0, block]) + up32(xf[3, block])
            if wave in (1, 2, 3):
                way = (block + 1) % 2
                chain[way].wait_recv()
                if wave > 1 or way == 0:
                    low = low + up32(zl[way, wave - 1, :, lo])
                if wave > 1 or way == 1:
                    high = high + up32(zl[way, wave - 1, :, hi])
            if wave == 4:
                for way in (0, 1):
                    chain[way].wait_recv()
                    low = low + up32(zl[way, 3, :, lo])
                    high = high + up32(zl[way, 3, :, hi])
                out_ref[:, lo] = low.astype(BF16)
                out_ref[:, hi] = high.astype(BF16)
                continue
            zb[block, :, lo] = low.astype(BF16)
            zb[block, :, hi] = high.astype(BF16)
            if wave == 0:
                chain[0] = send(zb.at[0, :, lo], zl.at[0, 0, :, lo], at(az=1))
                chain[1] = send(zb.at[0, :, hi], zl.at[1, 0, :, hi], at(az=-1))
            else:
                chain[way] = send(zb.at[block], zl.at[way, wave], at(az=1 if way == 0 else -1))

    running = [work(index) for index in range(len(GROUPS))] + [stream(), norm()]
    for name in ORDER:
        next(running[name], None)

    for copy in started[-POOL:]:
        copy.wait_send()


def local(tokens, norm_gain, gate_weight, up_weight, down_weight):
    vmem = pl.BlockSpec(memory_space=pltpu.VMEM)
    hbm = pl.BlockSpec(memory_space=pl.ANY)
    return pl.pallas_call(
        kernel,
        out_shape=jax.ShapeDtypeStruct((64, 1024), BF16),
        in_specs=[vmem, vmem, hbm, hbm, hbm],
        out_specs=vmem,
        scratch_shapes=[
            pltpu.VMEM((1024, 1792), BF16),
            pltpu.VMEM((896, 1024), BF16),
            pltpu.VMEM((256, 256), BF16),
            pltpu.VMEM((8, 256, 1024), BF16),
            pltpu.VMEM((8, 2, 4, 32, 1792), BF16),
            pltpu.VMEM((8, 4, 32, 1792), BF16),
            pltpu.VMEM((2, 8, 32, 896), BF16),
            pltpu.VMEM((4, 8, 32, 896), BF16),
            pltpu.VMEM((2, 8, 32, 896), BF16),
            pltpu.VMEM((8, 2, 4, 32, 896), BF16),
            pltpu.VMEM((8, 4, 64, 1024), BF16),
            pltpu.VMEM((2, 8, 64, 512), BF16),
            pltpu.VMEM((4, 8, 64, 512), BF16),
            pltpu.VMEM((8, 64, 1024), BF16),
            pltpu.VMEM((2, 4, 64, 1024), BF16),
            pltpu.VMEM((4, 8, 256), F32),
            pltpu.VMEM((3, 8, 256), F32),
            pltpu.VMEM((4, 8, 256), F32),
            pltpu.VMEM((8, 8, 256), F32),
            pltpu.SemaphoreType.DMA((3,)),
            pltpu.SemaphoreType.DMA((POOL,)),
            pltpu.SemaphoreType.DMA((COPIES,)),
        ],
        compiler_params=pltpu.CompilerParams(
            collective_id=0, has_side_effects=True, vmem_limit_bytes=58 * 2**20
        ),
        cost_estimate=pl.CostEstimate(flops=11_300_000_000, bytes_accessed=6_000_000, transcendentals=230_000),
        name="swiglu_block",
    )(tokens, norm_gain, gate_weight, up_weight, down_weight)


def solution(mesh):
    return jax.shard_map(
        local,
        mesh=mesh,
        in_specs=(P("row", "col"), P(), P("row", "col"), P("row", "col"), P("col", "row")),
        out_specs=P("col", "row"),
        check_vma=False,
    )
```

time: 124 us -> 99.6 us (0.80); the launches traced: 122 us -> 99.5 us
  Pallas kernels: 119 us -> 98 us
  local copies, waits for them, and re-layouts: 2.95 us -> 1.57 us
    pallas_call x1, Pallas kernels: 119 us -> 98 us  [local(): pl.pallas_call(kernel, out_shape=jax.ShapeDtypeStruct((64, 1024), BF16),...]
    reshape x1 -> x0, local copies, waits for them, and re-layouts: 1.38 us -> none  [local(): norm_gain.reshape(32, 256)]
where the time goes in v3:
time: 99.6 us; the launch traced here: 99.5 us
  Pallas kernels  98 us (98%)
  local copies, waits for them, and re-layouts  1.57 us (2%)
    pallas_call x1, Pallas kernels, local(): pl.pallas_call(kernel, out_shape=jax.ShapeDtypeStruct((64, 1024), BF16),...  98 us

profile of v3, /device:TPU:1, one launch (start us, length us, event | category | flops | bytes accessed | tf_op | source)
XLA Modules:
  0.0 99.5 jit_solution(13696398443945369291)
XLA Ops:
  0.0 98.0 %swiglu_block.1 = bf16[64,1024]{1,0:T(8,128)(2,1)} custom-call(bf16[256,256]{1,0:T(8,128)(2,1)} %tok_ref.1, f32[8192]{0:T(1024)} %gain_ref.1, bf16[1024,896]{1,0:T(8,128)(2,1)} %gate_hbm.1, bf16[1024,896]{1,0:T(8,128)(2,1)} %up_hbm.1, bf16[896,1024]{1,0:T(8,128)(2,1)} %down_hbm.1), custom_call_target="tpu_custom_call" | custom-call | flops 11299999744 | bytes 6000000 | tf_op jit(solution)/shard_map/swiglu_block/pallas_call | solution.py:349
  98.0 1.6 %copy.7 = bf16[64,1024]{1,0:T(8,128)(2,1)} copy(bf16[64,1024]{1,0:T(8,128)(2,1)} %swiglu_block.1) | data formatting | bytes 262144

commit v4 on v3

--- a/solution.py
+++ b/solution.py
@@ -28,8 +28,8 @@
     2, 4, 7, 5, 6, 3, 1, 4, 3, 5, 2, 6, 7, 4, 1, 5, 4, 6, 3, 7, 2, 5, 4, 6,
     5, 7, 3, 6, 4, 6, 5, 7, 7, 6, 7, 5, 6, 7, 7,
 )
-COPIES = 260
-POOL = 48
+COPIES = 140
+POOL = 24
 WIDE = 96
 
 
@@ -69,14 +69,22 @@
         load.start()
 
     started = []
-
-    def send(src, dst, device):
+    used = [0]
+
+    def arrival():
+        used[0] += 1
+        return recv_sems.at[used[0] - 1]
+
+    def wait_for(sem, view):
+        pltpu.make_async_copy(view, view, sem).wait()
+
+    def send(src, dst, device, sem=None):
         index = len(started)
         if index >= POOL:
             started[index - POOL].wait_send()
         copy = pltpu.make_async_remote_copy(
             src_ref=src, dst_ref=dst,
-            send_sem=send_sems.at[index % POOL], recv_sem=recv_sems.at[index],
+            send_sem=send_sems.at[index % POOL], recv_sem=arrival() if sem is None else sem,
             device_id=device, device_id_type=MESH,
         )
         copy.start()
@@ -105,10 +113,11 @@
     def norm():
         yield
         square_move.wait_recv()
-        sends = [send(ss.at[1], sx.at[i - 1], at(ax=i)) for i in (1, 2, 3)]
-        yield
-        for copy in sends:
-            copy.wait_recv()
+        sem = arrival()
+        for i in (1, 2, 3):
+            send(ss.at[1], sx.at[i - 1], at(ax=i), sem)
+        yield
+        wait_for(sem, sx)
         ss[2] = ss[1] + sx[0] + sx[1] + sx[2]
         copy = send(ss.at[2], sy.at[3], partner)
         yield
@@ -142,8 +151,10 @@
         wide, narrow = pl.ds(0, WIDE), pl.ds(WIDE, 256 - WIDE)
 
         def over_x(blocks, part):
-            view = xs.at[blocks, part, mine]
-            return [send(view, view, at(ax=i)) for i in (1, 3, 2)]
+            view, sem = xs.at[blocks, part, mine], arrival()
+            for i in (1, 3, 2):
+                send(view, view, at(ax=i), sem)
+            return lambda: wait_for(sem, xs.at[blocks, part, 0:768])
 
         def halves(first, size):
             return pl.ds(first, size // 2), pl.ds(first + size // 2, size // 2)
@@ -170,27 +181,24 @@
             move.wait_recv()
             if move is moves[0]:
                 gathered = over_x(0, wide)
-        if WIDE < 256:
-            forward(0, narrow, mine)
-            arrivals[0] = over_x(0, narrow)
-        yield
-        for copy in gathered:
-            copy.wait_recv()
+        forward(0, narrow, mine)
+        arrivals[0] = over_x(0, narrow)
+        yield
+        gathered()
         forward(0, wide, everything)
         for wave in (1, 2, 3, 4):
-            if WIDE < 256:
-                if wave < 4:
-                    forward(wave, narrow, mine)
-                else:
-                    for copy in ring[WIDE]:
-                        copy.wait_recv()
-                for group, (arrival, first, n) in enumerate(GROUPS):
-                    if arrival == wave:
-                        arrivals[group] = over_x(pl.ds(first, n), narrow)
+            if wave < 4:
+                forward(wave, narrow, mine)
+            else:
+                for copy in ring[WIDE]:
+                    copy.wait_recv()
+            for group, (arrives, first, n) in enumerate(GROUPS):
+                if arrives == wave:
+                    arrivals[group] = over_x(pl.ds(first, n), narrow)
             if wave < 4:
                 yield
                 forward(wave, wide, everything)
-        arrivals[len(GROUPS) - 1] = arrivals.get(len(GROUPS) - 1, []) + ring[0]
+        arrivals["last"] = ring[0]
 
     def gate_up(blocks, n, half, count):
         def tile(i, carry):
@@ -222,8 +230,10 @@
     def work(index):
         wave, first, n = GROUPS[index]
         blocks = pl.ds(first, n)
-        for copy in arrivals.get(index, []):
-            copy.wait_recv()
+        arrivals[index]()
+        if wave == 4:
+            for copy in arrivals["last"]:
+                copy.wait_recv()
         if index == 0:
             loads[0].wait()
             loads[1].wait()
@@ -241,21 +251,20 @@
         right = send(g.at[blocks, k, far, :, lo], yl.at[0, blocks], at(ay=1))
         left = send(g.at[blocks, k, far, :, hi], yl.at[1, blocks], at(ay=-1))
         add_pair(ahead)
-        plain_right = send(g.at[blocks, k, ahead, :, hi], yf.at[0, blocks], at(ay=1))
+        final = arrival()
+        send(g.at[blocks, k, ahead, :, hi], yf.at[0, blocks], at(ay=1), final)
         add_pair(behind)
-        plain_left = send(g.at[blocks, k, behind, :, lo], yf.at[1, blocks], at(ay=-1))
+        send(g.at[blocks, k, behind, :, lo], yf.at[1, blocks], at(ay=-1), final)
         add_pair(y)
         yield
         right.wait_recv()
         comb[0, blocks] = (up32(g[blocks, k, ahead, :, lo]) + up32(yl[0, blocks])).astype(BF16)
-        right = send(comb.at[0, blocks], yf.at[2, blocks], at(ay=1))
+        send(comb.at[0, blocks], yf.at[2, blocks], at(ay=1), final)
         left.wait_recv()
         comb[1, blocks] = (up32(g[blocks, k, behind, :, hi]) + up32(yl[1, blocks])).astype(BF16)
-        left = send(comb.at[1, blocks], yf.at[3, blocks], at(ay=-1))
-        yield
-        sums = [plain_right, plain_left, right, left]
-        for copy in sums:
-            copy.wait_recv()
+        send(comb.at[1, blocks], yf.at[3, blocks], at(ay=-1), final)
+        yield
+        wait_for(final, yf.at[:, blocks])
         for block in range(first, first + n):
             factor = factors(block)
             gate, up = up32(g[block, k, y, :, lo]), up32(g[block, k, y, :, hi])
@@ -263,12 +272,12 @@
             up = (up + up32(yf[0, block]) + up32(yf[3, block])) * factor
             h[block, k, y] = (gate / (1.0 + jnp.exp(-gate)) * up).astype(BF16)
         view = h.at[blocks, k, y]
-        pairs = []
+        pairs, across = arrival(), arrival()
 
         def to_partner(*places):
             for yy in places:
                 view = h.at[blocks, k, yy]
-                pairs.append(send(view, view, partner))
+                send(view, view, partner, pairs)
 
         right = send(view, view, at(ay=1))
         left = send(view, view, at(ay=-1))
@@ -276,38 +285,35 @@
         yield
         right.wait_recv()
         view = h.at[blocks, k, behind, pl.ds(0, 16)]
-        next_right = send(view, view, at(ay=1))
+        send(view, view, at(ay=1), across)
         left.wait_recv()
         view = h.at[blocks, k, ahead, pl.ds(16, 16)]
-        next_left = send(view, view, at(ay=-1))
+        send(view, view, at(ay=-1), across)
         to_partner(behind, ahead)
         yield
-        next_right.wait_recv()
-        next_left.wait_recv()
+        wait_for(across, h.at[blocks, k, far])
         to_partner(far)
         if index == 0:
             loads[2].wait()
         down(blocks, n, k)
         yield
-        for copy in pairs:
-            copy.wait_recv()
+        wait_for(pairs, h.at[blocks, 1 - k])
         down(blocks, n, 1 - k)
         lo, hi = pl.ds(0, 512), pl.ds(512, 512)
         right = send(o.at[blocks, far_x, :, lo], xd.at[0, blocks], at(ax=1))
         left = send(o.at[blocks, far_x, :, hi], xd.at[1, blocks], at(ax=-1))
-        plain_right = send(o.at[blocks, right_x, :, hi], xf.at[0, blocks], at(ax=1))
-        plain_left = send(o.at[blocks, left_x, :, lo], xf.at[1, blocks], at(ax=-1))
+        final = arrival()
+        send(o.at[blocks, right_x, :, hi], xf.at[0, blocks], at(ax=1), final)
+        send(o.at[blocks, left_x, :, lo], xf.at[1, blocks], at(ax=-1), final)
         yield
         right.wait_recv()
         o[blocks, right_x, :, lo] = (up32(o[blocks, right_x, :, lo]) + up32(xd[0, blocks])).astype(BF16)
-        right = send(o.at[blocks, right_x, :, lo], xf.at[2, blocks], at(ax=1))
+        send(o.at[blocks, right_x, :, lo], xf.at[2, blocks], at(ax=1), final)
         left.wait_recv()
         o[blocks, left_x, :, hi] = (up32(o[blocks, left_x, :, hi]) + up32(xd[1, blocks])).astype(BF16)
-        left = send(o.at[blocks, left_x, :, hi], xf.at[3, blocks], at(ax=-1))
-        yield
-        sums = [plain_right, plain_left, right, left]
-        for copy in sums:
-            copy.wait_recv()
+        send(o.at[blocks, left_x, :, hi], xf.at[3, blocks], at(ax=-1), final)
+        yield
+        wait_for(final, xf.at[:, blocks])
         for block in range(first, first + n):
             low, high = up32(o[block, x, :, lo]), up32(o[block, x, :, hi])
             low = low + up32(xf[1, block]) + up32(xf[2, block])
@@ -339,6 +345,7 @@
     for name in ORDER:
         next(running[name], None)
 
+    assert used[0] <= COPIES
     for copy in started[-POOL:]:
         copy.wait_send()
 

time: 99.6 us -> 98.4 us (0.988)
  Pallas kernels: 98 us -> 96.7 us
    pallas_call x1, Pallas kernels: 98 us -> 96.7 us  [local(): pl.pallas_call(kernel, out_shape=jax.ShapeDtypeStruct((64, 1024), BF16),...]
where the time goes in v4:
time: 98.4 us; the launch traced here: 98.3 us
  Pallas kernels  96.7 us (98%)
  local copies, waits for them, and re-layouts  1.57 us (2%)
    pallas_call x1, Pallas kernels, local(): pl.pallas_call(kernel, out_shape=jax.ShapeDtypeStruct((64, 1024), BF16),...  96.7 us

profile of v4, /device:TPU:1, one launch (start us, length us, event | category | flops | bytes accessed | tf_op | source)
XLA Modules:
  0.0 98.3 jit_solution(11062967664797466586)
XLA Ops:
  0.0 96.7 %swiglu_block.1 = bf16[64,1024]{1,0:T(8,128)(2,1)} custom-call(bf16[256,256]{1,0:T(8,128)(2,1)} %tok_ref.1, f32[8192]{0:T(1024)} %gain_ref.1, bf16[1024,896]{1,0:T(8,128)(2,1)} %gate_hbm.1, bf16[1024,896]{1,0:T(8,128)(2,1)} %up_hbm.1, bf16[896,1024]{1,0:T(8,128)(2,1)} %down_hbm.1), custom_call_target="tpu_custom_call" | custom-call | flops 11299999744 | bytes 6000000 | tf_op jit(solution)/shard_map/swiglu_block/pallas_call | solution.py:356
  96.7 1.6 %copy.7 = bf16[64,1024]{1,0:T(8,128)(2,1)} copy(bf16[64,1024]{1,0:T(8,128)(2,1)} %swiglu_block.1) | data formatting | bytes 262144
